TPU v7x, 32 devices: a whole 2x2x4 slice. The times are simulated.
32 devices in a mesh: district: 2 (over x), tile: 16 (over z, y, core).
Axes of the slice: x: 2, y: 2, z: 4, core: 2. Of those that a mesh axis runs over, the one named last changes fastest.
Arguments:
- cotangent: bfloat16 [384, 49152], P('tile', 'district'), parts along dimension 1, may hold values from -6 to 6
- coeffs: bfloat16 [2305, 49152], P(None, ('district', 'tile')), parts along dimension 1, may hold values from -0.0390625 to 0.0390625
- ctf: float32 [8, 24], replicated, may hold values from -1.5 to 1.5
- tap_count: int32 [8], replicated, may hold values from 1 to 24, as said below
- construction: int32 [49152], P('district'), parts along dimension 0, may hold values from 0 to 7
Outputs:
- sky_grad: float32 [384, 4610], P('tile', 'district'), parts along dimension 1
There are 2 independent parts, one for each index of `district`. A program takes and returns all parts, laid end to end along the dimension named above; an argument that names none is the same for every part. Nothing has to cross between parts.
Inputs may be any that keep to these rules, and one draw needn't show every extreme that they name: `tap_count`: some type has 24 live taps and some has one.
All inputs are finite; a program needn't handle non-finite values.
Results may differ from a plain program's by a relative error of at most 0.0029.
Values may be sent and summed in bfloat16 or wider, within the bound.
A program may use at most 128 MiB of HBM per device.

v0:
```python
import jax
import jax.numpy as jnp
from jax import lax
from jax.sharding import PartitionSpec as P


def shifted(value, axis, by):
    size = lax.axis_size(axis)
    pairs = [(i, i + by) for i in range(size) if 0 <= i + by < size]
    return lax.ppermute(value, axis, pairs)


def taps_table(kinds, tap_count, ctf):
    onehot = (kinds[:, None] == jnp.arange(ctf.shape[0], dtype=jnp.int32)[None, :]).astype(
        jnp.float32
    )
    live = jnp.where(
        jnp.arange(ctf.shape[1], dtype=jnp.int32)[None, :] < tap_count[:, None],
        ctf,
        jnp.float32(0.0),
    )
    return jnp.einsum("sc,ck->ks", onehot, live, precision=lax.Precision.HIGHEST)


def correlate(extended, taps, length):
    accum = jnp.zeros((length, extended.shape[1]), jnp.float32)
    for shift_k in range(taps.shape[0]):
        accum = accum + taps[shift_k][None, :] * extended[shift_k : shift_k + length].astype(
            jnp.float32
        )
    return accum.astype(jnp.bfloat16)


def per_device(cotangent, coeffs, ctf, tap_count, construction):
    span = ctf.shape[1]
    hours = cotangent.shape[0]
    taps = taps_table(construction, tap_count, ctf)
    tail = shifted(cotangent[: span - 1], "tile", -1)
    extended = jnp.concatenate([cotangent, tail], 0)
    surface = correlate(extended, taps, hours)
    by_points = lax.all_to_all(surface, "tile", split_axis=1, concat_axis=0, tiled=True)
    partial_value = lax.dot_general(
        by_points, coeffs, (((1,), (1,)), ((), ())), preferred_element_type=jnp.float32
    )
    return lax.psum_scatter(partial_value, "tile", scatter_dimension=0, tiled=True)


def solution(mesh):
    return jax.shard_map(
        per_device,
        mesh=mesh,
        in_specs=(P("tile", "district"), P(None, ("district", "tile")), P(), P(), P("district")),
        out_specs=P("tile", "district"),
        check_vma=False,
    )
```

profile of v0, /device:TPU:0, one launch (start us, length us, event | category | flops | bytes accessed | tf_op | source)
XLA Modules:
  0.0 148.4 jit_solution(18111956519017167114)
XLA Ops:
  6.5 0.0 reduce-scatter.4.cloned.1.call-start
  6.5 1.3 collective-permute-start
  7.8 2.1 %fusion = f32[24,24576]{1,0:T(8,128)S(1)} fusion(s32[24576]{0:T(1024)} %param.9, f32[8,24]{1,0:T(8,128)} %param.7, s32[8]{0:T(128)} %param.8), kind=kOutput, calls=%fused_computation.3 | convolution fusion | flops 56820096 | bytes 2458400 | tf_op jit(solution)/shard_map/sc,ck->ks/dot_general | solution.py:22
  9.9 0.0 copy-start
  10.0 1.6 %fusion.6 = (f32[1,24576]{1,0:T(1,128)S(1)}, f32[1,24576]{1,0:T(1,128)S(1)}, f32[1,24576]{1,0:T(1,128)S(1)}, f32[1,24576]{1,0:T(1,128)S(1)}, f32[1,24576]{1,0:T(...) fusion(f32[24,24576]{1,0:T(8,128)S(1)} %fusion), kind=kLoop, calls=%fused_computation.12 | loop fusion | bytes 3735552 | tf_op jit(solution)/shard_map/slice | solution.py:28
  11.6 0.4 fusion.7
  12.0 0.0 copy-done
  12.0 0.1 constant_dynamic-update-slice_fusion.1
  12.0 0.0 collective-permute-done
  12.1 0.0 slice-start
  12.1 0.1 constant_dynamic-update-slice_fusion
  12.2 0.0 slice-start.1
  12.2 7.4 %add_convert_fusion = bf16[24,24576]{1,0:T(8,128)(2,1)S(1)} fusion(bf16[24,24576]{1,0:T(8,128)(2,1)S(1)} %copy-done, bf16[47,24576]{1,0:T(8,128)(2,1)S(1)} %constant_dynamic-update-slice_fusion, f32[24576]{0:T(1024)S(1)} %bitcast.40, f32[24576]{0:T(1024)S(1)} %bitcast.41, f32[24576]{0:T(1024)S(1)} %bitcast.42, f32[24576]{0:T(1024)S(1)} %bitcast.43, ...), kind=kLoop, calls=%fused_computation | loop fusion | flops 42467328 | bytes 31850496 | tf_op jit(solution)/shard_map/convert_element_type | solution.py:31
  19.6 0.1 copy.11
  19.7 48.2 %all_to_all.19 = bf16[24,16,1536]{2,0,1:T(8,128)(2,1)S(1)} all-to-all(bf16[24,16,1536]{2,0,1:T(8,128)(2,1)S(1)} %bitcast.37), channel_id=1, replica_groups=mesh['district'=2,'tile'=16] {'tile'}, dimensions={1} | all-to-all | bytes 2359296 | tf_op jit(solution)/shard_map/all_to_all | solution.py:41
  67.9 0.0 slice-done
  67.9 0.0 slice-done.1
  67.9 5.1 %fusion.8 = f32[384,2305]{1,0:T(8,128)} fusion(bf16[384,1536]{1,0:T(8,128)(2,1)S(1)} %bitcast.38, bf16[2305,1536]{1,0:T(8,128)(2,1)S(1)} %bitcast.64), kind=kOutput, calls=%fused_computation.14 | convolution fusion | flops 2719088640 | bytes 11801088 | tf_op jit(solution)/shard_map/dot_general | solution.py:42
  72.9 0.0 reduce-scatter.4.cloned.1.call-update
  73.0 68.6 %reduce-scatter.4.cloned.1.call-done = f32[24,2305]{1,0:T(8,128)} async-done(((f32[384,2305]{1,0:T(8,128)}), f32[24,2305]{1,0:T(8,128)}) %reduce-scatter.4.cloned.1.call-update) | async-done | bytes 221296
  (1 shorter events, 0.0 us)
Async XLA Ops:
  6.5 135.0 %reduce-scatter.4.cloned.1.call-start = ((), (), s32[]{:S(2)}) async-start(), calls=%async_computation.2 | async-start | bytes 3969024
  6.5 5.5 %collective-permute-start = (bf16[23,24576]{1,0:T(8,128)(2,1)}, bf16[23,24576]{1,0:T(8,128)(2,1)S(1)}, u32[]{:S(2)}, u32[]{:S(2)}) collective-permute-start(bf16[23,24576]{1,0:T(8,128)(2,1)} %bitcast.35), channel_id=1, source_target_pairs={{1,0},{2,1},{3,2},{4,3},{5,4},{6,5},{7,6},{8,7},{9,8},{10,9},{11,1... | collective-permute-start | bytes 3391496 | tf_op jit(solution)/shard_map/ppermute | solution.py:10
  9.9 2.0 %copy-start = (bf16[24,24576]{1,0:T(8,128)(2,1)S(1)}, bf16[24,24576]{1,0:T(8,128)(2,1)}, u32[]{:S(2)}) copy-start(bf16[24,24576]{1,0:T(8,128)(2,1)} %param.5) | copy-start | bytes 3538948
  12.1 55.8 %slice-start = ((s8[7102464]{0:T(1024)(128)(4,1)}), s8[4194304]{0:T(1024)(128)(4,1)S(1)}, s32[]{:S(2)}) async-start(s8[7102464]{0:T(1024)(128)(4,1)} %bitcast.63), calls=%async_computation.3 | async-start | bytes 8388608
  12.2 55.7 %slice-start.1 = ((s8[7102464]{0:T(1024)(128)(4,1)}), s8[2908160]{0:T(1024)(128)(4,1)S(1)}, s32[]{:S(2)}) async-start(s8[7102464]{0:T(1024)(128)(4,1)} %bitcast.63), calls=%async_computation.4 | async-start | bytes 5816320
Sparse Core Ops, SparseCore 0:
  73.1 68.3 reduce-scatter.3
where the time goes:
time: 149 us; the launch traced here: 148 us
  waiting for transfers between devices  68.6 us (46%)
  blocking collectives  48.2 us (32%)
  between operations  13.5 us (9%)
  other arithmetic  7.44 us (5%)
  matrix products  7.16 us (5%)
  local copies, waits for them, and re-layouts  2.24 us (2%)
    unnamed x2, waiting for transfers between devices  68.6 us
    all_to_all x1, blocking collectives, per_device(): lax.all_to_all(surface, 'tile', split_axis=1, concat_axis=0, tiled=True)  48.2 us
    convert_element_type x1, other arithmetic, correlate(): return accum.astype(jnp.bfloat16)  7.44 us
    dot_general x1, matrix products, per_device(): lax.dot_general(by_points, coeffs, (((1,), (1,)), ((), ())), preferred_el...  5.05 us
  transfers between devices with their start and end apart: 2, of which 1 were waited for; matrix products, arithmetic and copies ran while one was open for 3% of the time, Pallas kernels for 0%

commit v1 on v0

--- a/solution.py
+++ b/solution.py
@@ -2,6 +2,22 @@
 import jax.numpy as jnp
 from jax import lax
 from jax.sharding import PartitionSpec as P
+
+
+def swapped_with_each(x, axis, split, join):
+    ways, here = (lax.axis_size(axis), lax.axis_index(axis))
+    width = x.shape[split] // ways
+    shape = list(x.shape)
+    shape[split] = width
+    height = shape[join]
+    shape[join] = height * ways
+    full = jnp.zeros(shape, x.dtype)
+    for mask in range(ways):
+        part = lax.dynamic_slice_in_dim(x, (here ^ mask) * width, width, axis=split)
+        if mask:
+            part = lax.ppermute(part, axis, [(d, d ^ mask) for d in range(ways)])
+        full = lax.dynamic_update_slice_in_dim(full, part, (here ^ mask) * height, axis=join)
+    return full
 
 
 def shifted(value, axis, by):
@@ -38,7 +54,7 @@
     tail = shifted(cotangent[: span - 1], "tile", -1)
     extended = jnp.concatenate([cotangent, tail], 0)
     surface = correlate(extended, taps, hours)
-    by_points = lax.all_to_all(surface, "tile", split_axis=1, concat_axis=0, tiled=True)
+    by_points = swapped_with_each(surface, "tile", 1, 0)
     partial_value = lax.dot_general(
         by_points, coeffs, (((1,), (1,)), ((), ())), preferred_element_type=jnp.float32
     )

time: 149 us -> 156 us (1.047)
  blocking collectives: 48.2 us -> 0 us
  starting transfers between devices: 1.28 us -> 40 us
  waiting for transfers between devices: 68.6 us -> 78.8 us
  local copies, waits for them, and re-layouts: 2.24 us -> 5.63 us
  matrix products: 7.16 us -> 10.2 us
    all_to_all x1 -> x0, blocking collectives: 48.2 us -> none  [per_device(): lax.all_to_all(surface, 'tile', split_axis=1, concat_axis=0, tiled=True)]
    ppermute x0 -> x15, starting transfers between devices: none -> 38.7 us  [swapped_with_each(): part = lax.ppermute(part, axis, [(d, d ^ mask) for d in range(ways)])]
    ppermute x0 -> x15, waiting for transfers between devices: none -> 7.34 us  [swapped_with_each(): part = lax.ppermute(part, axis, [(d, d ^ mask) for d in range(ways)])]
    dot_general x1, matrix products: 5.05 us -> 8.1 us  [per_device(): lax.dot_general(by_points, coeffs, (((1,), (1,)), ((), ())), preferred_el...]
    unnamed x2, waiting for transfers between devices: 68.6 us -> 71.4 us
  transfers between devices with their start and end apart: 2 -> 17, of which waited for: 1 -> 5; matrix products, arithmetic and copies ran while one was open for 3% -> 4% of each run, Pallas kernels for 0% -> 0%
where the time goes in v1:
time: 156 us
  waiting for transfers between devices  78.8 us (51%)
  starting transfers between devices  40 us (26%)
  between operations  14.1 us (9%)
  matrix products  10.2 us (7%)
  other arithmetic  7.42 us (5%)
  local copies, waits for them, and re-layouts  5.63 us (4%)
    unnamed x2, waiting for transfers between devices  71.4 us
    ppermute x15, starting transfers between devices, swapped_with_each(): part = lax.ppermute(part, axis, [(d, d ^ mask) for d in range(ways)])  38.7 us
    dot_general x1, matrix products, per_device(): lax.dot_general(by_points, coeffs, (((1,), (1,)), ((), ())), preferred_el...  8.1 us
    convert_element_type x1, other arithmetic, correlate(): return accum.astype(jnp.bfloat16)  7.42 us
    ppermute x15, waiting for transfers between devices, swapped_with_each(): part = lax.ppermute(part, axis, [(d, d ^ mask) for d in range(ways)])  7.34 us
    slice x2, local copies, waits for them, and re-layouts, correlate(): taps[shift_k][None, :]  3.46 us
  transfers between devices with their start and end apart: 17, of which 5 were waited for; matrix products, arithmetic and copies ran while one was open for 4% of the time, Pallas kernels for 0%

profile of v1, /device:TPU:0, one launch (start us, length us, event | category | flops | bytes accessed | tf_op | source)
XLA Modules:
  0.0 156.1 jit_solution(6899491524709529267)
XLA Ops:
  6.5 1.3 collective-permute-start
  7.8 2.1 %fusion = f32[24,24576]{1,0:T(8,128)S(1)} fusion(s32[24576]{0:T(1024)} %param.9, f32[8,24]{1,0:T(8,128)} %param.7, s32[8]{0:T(128)} %param.8), kind=kOutput, calls=%fused_computation.2 | convolution fusion | flops 56820096 | bytes 2458400 | tf_op jit(solution)/shard_map/sc,ck->ks/dot_general | solution.py:38
  9.9 0.0 copy-start
  10.0 2.3 %fusion.6 = (f32[1,24576]{1,0:T(1,128)}, f32[1,24576]{1,0:T(1,128)}, f32[1,24576]{1,0:T(1,128)}, f32[1,24576]{1,0:T(1,128)}, f32[1,24576]{1,0:T(1,128)}, /*index...) fusion(f32[24,24576]{1,0:T(8,128)S(1)} %fusion), kind=kLoop, calls=%fused_computation.42 | loop fusion | bytes 3735552 | tf_op jit(solution)/shard_map/slice | solution.py:44
  12.3 1.2 fusion.7
  13.4 0.1 constant_dynamic-update-slice_fusion.16
  13.6 0.0 copy-start.1
  13.8 0.0 collective-permute-done
  13.9 1.6 %constant_dynamic-update-slice_fusion.15 = bf16[47,24576]{1,0:T(8,128)(2,1)S(1)} fusion(bf16[47,24576]{1,0:T(8,128)(2,1)S(1)} %constant_dynamic-update-slice_fusion.16, bf16[23,24576]{1,0:T(8,128)(2,1)} %collective-permute-done), kind=kLoop, calls=%fused_computation.35 | loop fusion | bytes 2310144 | tf_op jit(solution)/shard_map/concatenate | solution.py:55
  15.4 0.0 copy-done.1
  15.4 0.0 copy-done.2
  15.5 0.0 copy-done.3
  15.5 0.0 copy-done.4
  15.5 0.0 copy-done.5
  15.5 0.0 copy-done.6
  15.5 0.0 copy-done.7
  15.5 0.0 copy-done.8
  15.5 0.0 copy-done.9
  15.5 0.0 copy-done.10
  15.5 0.0 copy-done.11
  15.5 0.0 copy-done.12
  15.6 0.0 copy-done.13
  15.6 0.0 copy-done.14
  15.6 0.0 copy-done.15
  15.6 0.0 copy-done.16
  15.6 0.0 copy-done.17
  15.7 0.0 copy-done.23
  15.7 0.0 copy-done.24
  15.7 7.4 %add_convert_fusion = bf16[24,24576]{1,0:T(8,128)(2,1)S(1)} fusion(bf16[24,24576]{1,0:T(8,128)(2,1)S(1)} %copy-done, bf16[47,24576]{1,0:T(8,128)(2,1)S(1)} %constant_dynamic-update-slice_fusion.15, f32[24576]{0:T(1024)S(1)} %bitcast.30, f32[24576]{0:T(1024)S(1)} %bitcast.31, f32[24576]{0:T(1024)S(1)} %bitcast.32, f32[24576]{0:T(1024)S(1)} %bitcast.33, ...), kind=kLoop, calls=%fused_computation | loop fusion | flops 42467328 | bytes 31850496 | tf_op jit(solution)/shard_map/convert_element_type | solution.py:47
  23.1 0.1 broadcast_in_dim.5
  23.2 0.2 constant_dynamic-slice_fusion
  23.4 11.7 %collective-permute-start.1 = (bf16[24,1536]{1,0:T(8,128)(2,1)S(1)}, bf16[24,1536]{1,0:T(8,128)(2,1)S(1)}, u32[]{:S(2)}, u32[]{:S(2)}) collective-permute-start(bf16[24,1536]{1,0:T(8,128)(2,1)S(1)} %get-tuple-element.43), channel_id=1, source_target_pairs={{0,1},{1,0},{2,3},{3,2},{4,5},{5,4},{6,7},{7,6},{8,9},{9,8},{10,11... | collective-permute-start | bytes 221192 | tf_op jit(solution)/shard_map/ppermute | solution.py:18
  35.1 2.4 %collective-permute-start.2 = (bf16[24,1536]{1,0:T(8,128)(2,1)S(1)}, bf16[24,1536]{1,0:T(8,128)(2,1)S(1)}, u32[]{:S(2)}, u32[]{:S(2)}) collective-permute-start(bf16[24,1536]{1,0:T(8,128)(2,1)S(1)} %get-tuple-element.42), channel_id=1, source_target_pairs={{0,2},{1,3},{2,0},{3,1},{4,6},{5,7},{6,4},{7,5},{8,10},{9,11},{10,... | collective-permute-start | bytes 221192 | tf_op jit(solution)/shard_map/ppermute | solution.py:18
  37.4 0.0 collective-permute-start.3
  37.4 1.6 %collective-permute-start.4 = (bf16[24,1536]{1,0:T(8,128)(2,1)S(1)}, bf16[24,1536]{1,0:T(8,128)(2,1)S(1)}, u32[]{:S(2)}, u32[]{:S(2)}) collective-permute-start(bf16[24,1536]{1,0:T(8,128)(2,1)S(1)} %get-tuple-element.40), channel_id=1, source_target_pairs={{0,4},{1,5},{2,6},{3,7},{4,0},{5,1},{6,2},{7,3},{8,12},{9,13},{10,... | collective-permute-start | bytes 221192 | tf_op jit(solution)/shard_map/ppermute | solution.py:18
  39.0 0.0 collective-permute-start.5
  39.0 0.0 collective-permute-done.1
  39.0 2.9 %collective-permute-start.6 = (bf16[24,1536]{1,0:T(8,128)(2,1)S(1)}, bf16[24,1536]{1,0:T(8,128)(2,1)S(1)}, u32[]{:S(2)}, u32[]{:S(2)}) collective-permute-start(bf16[24,1536]{1,0:T(8,128)(2,1)S(1)} %get-tuple-element.38), channel_id=1, source_target_pairs={{0,6},{1,7},{2,4},{3,5},{4,2},{5,3},{6,0},{7,1},{8,14},{9,15},{10,... | collective-permute-start | bytes 221192 | tf_op jit(solution)/shard_map/ppermute | solution.py:18
  42.0 0.0 collective-permute-done.2
  42.0 0.1 collective-permute-start.7
  42.1 0.0 collective-permute-done.3
  42.1 2.5 %collective-permute-start.8 = (bf16[24,1536]{1,0:T(8,128)(2,1)S(1)}, bf16[24,1536]{1,0:T(8,128)(2,1)S(1)}, u32[]{:S(2)}, u32[]{:S(2)}) collective-permute-start(bf16[24,1536]{1,0:T(8,128)(2,1)S(1)} %get-tuple-element.36), channel_id=1, source_target_pairs={{0,8},{1,9},{2,10},{3,11},{4,12},{5,13},{6,14},{7,15},{8,0},{9,1},... | collective-permute-start | bytes 221192 | tf_op jit(solution)/shard_map/ppermute | solution.py:18
  44.6 0.0 collective-permute-done.4
  44.6 1.5 collective-permute-start.9
  46.1 0.0 collective-permute-done.5
  46.1 2.5 %collective-permute-start.10 = (bf16[24,1536]{1,0:T(8,128)(2,1)S(1)}, bf16[24,1536]{1,0:T(8,128)(2,1)S(1)}, u32[]{:S(2)}, u32[]{:S(2)}) collective-permute-start(bf16[24,1536]{1,0:T(8,128)(2,1)S(1)} %get-tuple-element.34), channel_id=1, source_target_pairs={{0,10},{1,11},{2,8},{3,9},{4,14},{5,15},{6,12},{7,13},{8,2},{9,3},... | collective-permute-start | bytes 221192 | tf_op jit(solution)/shard_map/ppermute | solution.py:18
  48.6 0.0 collective-permute-done.6
  48.6 0.1 collective-permute-start.11
  48.7 0.5 collective-permute-done.7
  49.2 2.8 %collective-permute-start.12 = (bf16[24,1536]{1,0:T(8,128)(2,1)S(1)}, bf16[24,1536]{1,0:T(8,128)(2,1)S(1)}, u32[]{:S(2)}, u32[]{:S(2)}) collective-permute-start(bf16[24,1536]{1,0:T(8,128)(2,1)S(1)} %get-tuple-element.32), channel_id=1, source_target_pairs={{0,12},{1,13},{2,14},{3,15},{4,8},{5,9},{6,10},{7,11},{8,4},{9,5},... | collective-permute-start | bytes 221192 | tf_op jit(solution)/shard_map/ppermute | solution.py:18
  52.0 0.0 collective-permute-done.8
  52.0 6.6 %collective-permute-start.13 = (bf16[24,1536]{1,0:T(8,128)(2,1)S(1)}, bf16[24,1536]{1,0:T(8,128)(2,1)S(1)}, u32[]{:S(2)}, u32[]{:S(2)}) collective-permute-start(bf16[24,1536]{1,0:T(8,128)(2,1)S(1)} %get-tuple-element.31), channel_id=1, source_target_pairs={{0,13},{1,12},{2,15},{3,14},{4,9},{5,8},{6,11},{7,10},{8,5},{9,4},... | collective-permute-start | bytes 221192 | tf_op jit(solution)/shard_map/ppermute | solution.py:18
  58.5 0.0 collective-permute-done.9
  58.6 3.3 %collective-permute-start.14 = (bf16[24,1536]{1,0:T(8,128)(2,1)S(1)}, bf16[24,1536]{1,0:T(8,128)(2,1)S(1)}, u32[]{:S(2)}, u32[]{:S(2)}) collective-permute-start(bf16[24,1536]{1,0:T(8,128)(2,1)S(1)} %get-tuple-element.30), channel_id=1, source_target_pairs={{0,14},{1,15},{2,12},{3,13},{4,10},{5,11},{6,8},{7,9},{8,6},{9,7},... | collective-permute-start | bytes 221192 | tf_op jit(solution)/shard_map/ppermute | solution.py:18
  61.9 0.6 collective-permute-done.10
  62.5 0.9 collective-permute-start.15
  63.4 0.0 collective-permute-done.11
  63.4 0.0 collective-permute-done.12
  63.5 0.0 collective-permute-done.13
  63.5 2.3 %collective-permute-done.14 = bf16[24,1536]{1,0:T(8,128)(2,1)S(1)} collective-permute-done((bf16[24,1536]{1,0:T(8,128)(2,1)S(1)}, bf16[24,1536]{1,0:T(8,128)(2,1)S(1)}, u32[]{:S(2)}, u32[]{:S(2)}) %collective-permute-start.14) | collective-permute-done | bytes 73760 | tf_op jit(solution)/shard_map/ppermute | solution.py:18
  65.8 3.9 %collective-permute-done.15 = bf16[24,1536]{1,0:T(8,128)(2,1)S(1)} collective-permute-done((bf16[24,1536]{1,0:T(8,128)(2,1)S(1)}, bf16[24,1536]{1,0:T(8,128)(2,1)S(1)}, u32[]{:S(2)}, u32[]{:S(2)}) %collective-permute-start.15) | collective-permute-done | bytes 73760 | tf_op jit(solution)/shard_map/ppermute | solution.py:18
  69.7 8.1 %fusion.8 = f32[384,2305]{1,0:T(8,128)} fusion(bf16[384,1536]{1,0:T(8,128)(2,1)S(1)} %constant_dynamic-update-slice_fusion.14, bf16[2305,1536]{1,0:T(8,128)(2,1)} %param.6), kind=kOutput, calls=%fused_computation.44 | convolution fusion | flops 2719088640 | bytes 11801088 | tf_op jit(solution)/shard_map/dot_general | solution.py:58
  77.8 0.0 reduce-scatter.4.cloned.1.call-update
  77.9 71.4 %reduce-scatter.4.cloned.1.call-done = f32[24,2305]{1,0:T(8,128)} async-done(((f32[384,2305]{1,0:T(8,128)}), f32[24,2305]{1,0:T(8,128)}) %reduce-scatter.4.cloned.1.call-update) | async-done | bytes 221296
  (45 shorter events, 0.2 us)
Async XLA Ops:
  6.5 142.8 %reduce-scatter.4.cloned.1.call-start = ((), (), s32[]{:S(2)}) async-start(), calls=%async_computation.1 | async-start | bytes 3969024
  6.5 7.3 %collective-permute-start = (bf16[23,24576]{1,0:T(8,128)(2,1)}, bf16[23,24576]{1,0:T(8,128)(2,1)}, u32[]{:S(2)}, u32[]{:S(2)}) collective-permute-start(bf16[23,24576]{1,0:T(8,128)(2,1)} %bitcast.28), channel_id=1, source_target_pairs={{1,0},{2,1},{3,2},{4,3},{5,4},{6,5},{7,6},{8,7},{9,8},{10,9},{11,1... | collective-permute-start | bytes 3391496 | tf_op jit(solution)/shard_map/ppermute | solution.py:26
  9.9 3.5 %copy-start = (bf16[24,24576]{1,0:T(8,128)(2,1)S(1)}, bf16[24,24576]{1,0:T(8,128)(2,1)}, u32[]{:S(2)}) copy-start(bf16[24,24576]{1,0:T(8,128)(2,1)} %param.5) | copy-start | bytes 3538948
  13.6 1.8 %copy-start.1 = (f32[1,24576]{1,0:T(1,128)S(1)}, f32[1,24576]{1,0:T(1,128)}, u32[]{:S(2)}) copy-start(f32[1,24576]{1,0:T(1,128)} %get-tuple-element.5) | copy-start | bytes 294916
  13.6 1.8 %copy-start.2 = (f32[1,24576]{1,0:T(1,128)S(1)}, f32[1,24576]{1,0:T(1,128)}, u32[]{:S(2)}) copy-start(f32[1,24576]{1,0:T(1,128)} %get-tuple-element.6) | copy-start | bytes 294916
  13.6 1.8 %copy-start.3 = (f32[1,24576]{1,0:T(1,128)S(1)}, f32[1,24576]{1,0:T(1,128)}, u32[]{:S(2)}) copy-start(f32[1,24576]{1,0:T(1,128)} %get-tuple-element.7) | copy-start | bytes 294916
  13.6 1.8 %copy-start.4 = (f32[1,24576]{1,0:T(1,128)S(1)}, f32[1,24576]{1,0:T(1,128)}, u32[]{:S(2)}) copy-start(f32[1,24576]{1,0:T(1,128)} %get-tuple-element.8) | copy-start | bytes 294916
  13.6 1.8 %copy-start.5 = (f32[1,24576]{1,0:T(1,128)S(1)}, f32[1,24576]{1,0:T(1,128)}, u32[]{:S(2)}) copy-start(f32[1,24576]{1,0:T(1,128)} %get-tuple-element.9) | copy-start | bytes 294916
  13.7 1.8 %copy-start.6 = (f32[1,24576]{1,0:T(1,128)S(1)}, f32[1,24576]{1,0:T(1,128)}, u32[]{:S(2)}) copy-start(f32[1,24576]{1,0:T(1,128)} %get-tuple-element.10) | copy-start | bytes 294916
  13.7 1.8 %copy-start.7 = (f32[1,24576]{1,0:T(1,128)S(1)}, f32[1,24576]{1,0:T(1,128)}, u32[]{:S(2)}) copy-start(f32[1,24576]{1,0:T(1,128)} %get-tuple-element.11) | copy-start | bytes 294916
  13.7 1.8 %copy-start.8 = (f32[1,24576]{1,0:T(1,128)S(1)}, f32[1,24576]{1,0:T(1,128)}, u32[]{:S(2)}) copy-start(f32[1,24576]{1,0:T(1,128)} %get-tuple-element.12) | copy-start | bytes 294916
  13.7 1.8 %copy-start.9 = (f32[1,24576]{1,0:T(1,128)S(1)}, f32[1,24576]{1,0:T(1,128)}, u32[]{:S(2)}) copy-start(f32[1,24576]{1,0:T(1,128)} %get-tuple-element.13) | copy-start | bytes 294916
  13.7 1.8 %copy-start.10 = (f32[1,24576]{1,0:T(1,128)S(1)}, f32[1,24576]{1,0:T(1,128)}, u32[]{:S(2)}) copy-start(f32[1,24576]{1,0:T(1,128)} %get-tuple-element.14) | copy-start | bytes 294916
  13.7 1.8 %copy-start.11 = (f32[1,24576]{1,0:T(1,128)S(1)}, f32[1,24576]{1,0:T(1,128)}, u32[]{:S(2)}) copy-start(f32[1,24576]{1,0:T(1,128)} %get-tuple-element.15) | copy-start | bytes 294916
  13.7 1.8 %copy-start.12 = (f32[1,24576]{1,0:T(1,128)S(1)}, f32[1,24576]{1,0:T(1,128)}, u32[]{:S(2)}) copy-start(f32[1,24576]{1,0:T(1,128)} %get-tuple-element.16) | copy-start | bytes 294916
  13.7 1.8 %copy-start.13 = (f32[1,24576]{1,0:T(1,128)S(1)}, f32[1,24576]{1,0:T(1,128)}, u32[]{:S(2)}) copy-start(f32[1,24576]{1,0:T(1,128)} %get-tuple-element.17) | copy-start | bytes 294916
  13.7 1.8 %copy-start.14 = (f32[1,24576]{1,0:T(1,128)S(1)}, f32[1,24576]{1,0:T(1,128)}, u32[]{:S(2)}) copy-start(f32[1,24576]{1,0:T(1,128)} %get-tuple-element.18) | copy-start | bytes 294916
  13.7 1.8 %copy-start.15 = (f32[1,24576]{1,0:T(1,128)S(1)}, f32[1,24576]{1,0:T(1,128)}, u32[]{:S(2)}) copy-start(f32[1,24576]{1,0:T(1,128)} %get-tuple-element.19) | copy-start | bytes 294916
  13.8 1.8 %copy-start.16 = (f32[1,24576]{1,0:T(1,128)S(1)}, f32[1,24576]{1,0:T(1,128)}, u32[]{:S(2)}) copy-start(f32[1,24576]{1,0:T(1,128)} %get-tuple-element.20) | copy-start | bytes 294916
  13.8 1.8 %copy-start.17 = (f32[1,24576]{1,0:T(1,128)S(1)}, f32[1,24576]{1,0:T(1,128)}, u32[]{:S(2)}) copy-start(f32[1,24576]{1,0:T(1,128)} %get-tuple-element.21) | copy-start | bytes 294916
  13.8 1.8 %copy-start.18 = (f32[1,24576]{1,0:T(1,128)S(1)}, f32[1,24576]{1,0:T(1,128)}, u32[]{:S(2)}) copy-start(f32[1,24576]{1,0:T(1,128)} %get-tuple-element.22) | copy-start | bytes 294916
  13.8 1.8 %copy-start.19 = (f32[1,24576]{1,0:T(1,128)S(1)}, f32[1,24576]{1,0:T(1,128)}, u32[]{:S(2)}) copy-start(f32[1,24576]{1,0:T(1,128)} %get-tuple-element.23) | copy-start | bytes 294916
  13.8 1.8 %copy-start.20 = (f32[1,24576]{1,0:T(1,128)S(1)}, f32[1,24576]{1,0:T(1,128)}, u32[]{:S(2)}) copy-start(f32[1,24576]{1,0:T(1,128)} %get-tuple-element.24) | copy-start | bytes 294916
  13.8 1.8 %copy-start.21 = (f32[1,24576]{1,0:T(1,128)S(1)}, f32[1,24576]{1,0:T(1,128)}, u32[]{:S(2)}) copy-start(f32[1,24576]{1,0:T(1,128)} %get-tuple-element.25) | copy-start | bytes 294916
  13.8 1.8 %copy-start.22 = (f32[1,24576]{1,0:T(1,128)S(1)}, f32[1,24576]{1,0:T(1,128)}, u32[]{:S(2)}) copy-start(f32[1,24576]{1,0:T(1,128)} %get-tuple-element.26) | copy-start | bytes 294916
  13.8 1.8 %copy-start.23 = (f32[1,24576]{1,0:T(1,128)S(1)}, f32[1,24576]{1,0:T(1,128)}, u32[]{:S(2)}) copy-start(f32[1,24576]{1,0:T(1,128)} %get-tuple-element.27) | copy-start | bytes 294916
  13.8 1.9 %copy-start.24 = (f32[1,24576]{1,0:T(1,128)S(1)}, f32[1,24576]{1,0:T(1,128)}, u32[]{:S(2)}) copy-start(f32[1,24576]{1,0:T(1,128)} %get-tuple-element.28) | copy-start | bytes 294916
  23.4 15.6 %collective-permute-start.1 = (bf16[24,1536]{1,0:T(8,128)(2,1)S(1)}, bf16[24,1536]{1,0:T(8,128)(2,1)S(1)}, u32[]{:S(2)}, u32[]{:S(2)}) collective-permute-start(bf16[24,1536]{1,0:T(8,128)(2,1)S(1)} %get-tuple-element.43), channel_id=1, source_target_pairs={{0,1},{1,0},{2,3},{3,2},{4,5},{5,4},{6,7},{7,6},{8,9},{9,8},{10,11... | collective-permute-start | bytes 221192 | tf_op jit(solution)/shard_map/ppermute | solution.py:18
  35.1 6.9 %collective-permute-start.2 = (bf16[24,1536]{1,0:T(8,128)(2,1)S(1)}, bf16[24,1536]{1,0:T(8,128)(2,1)S(1)}, u32[]{:S(2)}, u32[]{:S(2)}) collective-permute-start(bf16[24,1536]{1,0:T(8,128)(2,1)S(1)} %get-tuple-element.42), channel_id=1, source_target_pairs={{0,2},{1,3},{2,0},{3,1},{4,6},{5,7},{6,4},{7,5},{8,10},{9,11},{10,... | collective-permute-start | bytes 221192 | tf_op jit(solution)/shard_map/ppermute | solution.py:18
  37.4 4.6 %collective-permute-start.3 = (bf16[24,1536]{1,0:T(8,128)(2,1)S(1)}, bf16[24,1536]{1,0:T(8,128)(2,1)S(1)}, u32[]{:S(2)}, u32[]{:S(2)}) collective-permute-start(bf16[24,1536]{1,0:T(8,128)(2,1)S(1)} %get-tuple-element.41), channel_id=1, source_target_pairs={{0,3},{1,2},{2,1},{3,0},{4,7},{5,6},{6,5},{7,4},{8,11},{9,10},{10,... | collective-permute-start | bytes 221192 | tf_op jit(solution)/shard_map/ppermute | solution.py:18
  37.4 7.2 %collective-permute-start.4 = (bf16[24,1536]{1,0:T(8,128)(2,1)S(1)}, bf16[24,1536]{1,0:T(8,128)(2,1)S(1)}, u32[]{:S(2)}, u32[]{:S(2)}) collective-permute-start(bf16[24,1536]{1,0:T(8,128)(2,1)S(1)} %get-tuple-element.40), channel_id=1, source_target_pairs={{0,4},{1,5},{2,6},{3,7},{4,0},{5,1},{6,2},{7,3},{8,12},{9,13},{10,... | collective-permute-start | bytes 221192 | tf_op jit(solution)/shard_map/ppermute | solution.py:18
  39.0 7.1 %collective-permute-start.5 = (bf16[24,1536]{1,0:T(8,128)(2,1)S(1)}, bf16[24,1536]{1,0:T(8,128)(2,1)S(1)}, u32[]{:S(2)}, u32[]{:S(2)}) collective-permute-start(bf16[24,1536]{1,0:T(8,128)(2,1)S(1)} %get-tuple-element.39), channel_id=1, source_target_pairs={{0,5},{1,4},{2,7},{3,6},{4,1},{5,0},{6,3},{7,2},{8,13},{9,12},{10,... | collective-permute-start | bytes 221192 | tf_op jit(solution)/shard_map/ppermute | solution.py:18
  39.0 9.6 %collective-permute-start.6 = (bf16[24,1536]{1,0:T(8,128)(2,1)S(1)}, bf16[24,1536]{1,0:T(8,128)(2,1)S(1)}, u32[]{:S(2)}, u32[]{:S(2)}) collective-permute-start(bf16[24,1536]{1,0:T(8,128)(2,1)S(1)} %get-tuple-element.38), channel_id=1, source_target_pairs={{0,6},{1,7},{2,4},{3,5},{4,2},{5,3},{6,0},{7,1},{8,14},{9,15},{10,... | collective-permute-start | bytes 221192 | tf_op jit(solution)/shard_map/ppermute | solution.py:18
  42.0 7.2 %collective-permute-start.7 = (bf16[24,1536]{1,0:T(8,128)(2,1)S(1)}, bf16[24,1536]{1,0:T(8,128)(2,1)S(1)}, u32[]{:S(2)}, u32[]{:S(2)}) collective-permute-start(bf16[24,1536]{1,0:T(8,128)(2,1)S(1)} %get-tuple-element.37), channel_id=1, source_target_pairs={{0,7},{1,6},{2,5},{3,4},{4,3},{5,2},{6,1},{7,0},{8,15},{9,14},{10,... | collective-permute-start | bytes 221192 | tf_op jit(solution)/shard_map/ppermute | solution.py:18
  42.1 9.9 %collective-permute-start.8 = (bf16[24,1536]{1,0:T(8,128)(2,1)S(1)}, bf16[24,1536]{1,0:T(8,128)(2,1)S(1)}, u32[]{:S(2)}, u32[]{:S(2)}) collective-permute-start(bf16[24,1536]{1,0:T(8,128)(2,1)S(1)} %get-tuple-element.36), channel_id=1, source_target_pairs={{0,8},{1,9},{2,10},{3,11},{4,12},{5,13},{6,14},{7,15},{8,0},{9,1},... | collective-permute-start | bytes 221192 | tf_op jit(solution)/shard_map/ppermute | solution.py:18
  44.6 13.9 %collective-permute-start.9 = (bf16[24,1536]{1,0:T(8,128)(2,1)S(1)}, bf16[24,1536]{1,0:T(8,128)(2,1)S(1)}, u32[]{:S(2)}, u32[]{:S(2)}) collective-permute-start(bf16[24,1536]{1,0:T(8,128)(2,1)S(1)} %get-tuple-element.35), channel_id=1, source_target_pairs={{0,9},{1,8},{2,11},{3,10},{4,13},{5,12},{6,15},{7,14},{8,1},{9,0},... | collective-permute-start | bytes 221192 | tf_op jit(solution)/shard_map/ppermute | solution.py:18
  46.1 16.4 %collective-permute-start.10 = (bf16[24,1536]{1,0:T(8,128)(2,1)S(1)}, bf16[24,1536]{1,0:T(8,128)(2,1)S(1)}, u32[]{:S(2)}, u32[]{:S(2)}) collective-permute-start(bf16[24,1536]{1,0:T(8,128)(2,1)S(1)} %get-tuple-element.34), channel_id=1, source_target_pairs={{0,10},{1,11},{2,8},{3,9},{4,14},{5,15},{6,12},{7,13},{8,2},{9,3},... | collective-permute-start | bytes 221192 | tf_op jit(solution)/shard_map/ppermute | solution.py:18
  48.6 14.8 %collective-permute-start.11 = (bf16[24,1536]{1,0:T(8,128)(2,1)S(1)}, bf16[24,1536]{1,0:T(8,128)(2,1)S(1)}, u32[]{:S(2)}, u32[]{:S(2)}) collective-permute-start(bf16[24,1536]{1,0:T(8,128)(2,1)S(1)} %get-tuple-element.33), channel_id=1, source_target_pairs={{0,11},{1,10},{2,9},{3,8},{4,15},{5,14},{6,13},{7,12},{8,3},{9,2},... | collective-permute-start | bytes 221192 | tf_op jit(solution)/shard_map/ppermute | solution.py:18
  49.2 14.2 %collective-permute-start.12 = (bf16[24,1536]{1,0:T(8,128)(2,1)S(1)}, bf16[24,1536]{1,0:T(8,128)(2,1)S(1)}, u32[]{:S(2)}, u32[]{:S(2)}) collective-permute-start(bf16[24,1536]{1,0:T(8,128)(2,1)S(1)} %get-tuple-element.32), channel_id=1, source_target_pairs={{0,12},{1,13},{2,14},{3,15},{4,8},{5,9},{6,10},{7,11},{8,4},{9,5},... | collective-permute-start | bytes 221192 | tf_op jit(solution)/shard_map/ppermute | solution.py:18
  52.0 11.5 %collective-permute-start.13 = (bf16[24,1536]{1,0:T(8,128)(2,1)S(1)}, bf16[24,1536]{1,0:T(8,128)(2,1)S(1)}, u32[]{:S(2)}, u32[]{:S(2)}) collective-permute-start(bf16[24,1536]{1,0:T(8,128)(2,1)S(1)} %get-tuple-element.31), channel_id=1, source_target_pairs={{0,13},{1,12},{2,15},{3,14},{4,9},{5,8},{6,11},{7,10},{8,5},{9,4},... | collective-permute-start | bytes 221192 | tf_op jit(solution)/shard_map/ppermute | solution.py:18
  58.6 7.2 %collective-permute-start.14 = (bf16[24,1536]{1,0:T(8,128)(2,1)S(1)}, bf16[24,1536]{1,0:T(8,128)(2,1)S(1)}, u32[]{:S(2)}, u32[]{:S(2)}) collective-permute-start(bf16[24,1536]{1,0:T(8,128)(2,1)S(1)} %get-tuple-element.30), channel_id=1, source_target_pairs={{0,14},{1,15},{2,12},{3,13},{4,10},{5,11},{6,8},{7,9},{8,6},{9,7},... | collective-permute-start | bytes 221192 | tf_op jit(solution)/shard_map/ppermute | solution.py:18
  62.5 7.2 %collective-permute-start.15 = (bf16[24,1536]{1,0:T(8,128)(2,1)S(1)}, bf16[24,1536]{1,0:T(8,128)(2,1)S(1)}, u32[]{:S(2)}, u32[]{:S(2)}) collective-permute-start(bf16[24,1536]{1,0:T(8,128)(2,1)S(1)} %get-tuple-element.29), channel_id=1, source_target_pairs={{0,15},{1,14},{2,13},{3,12},{4,11},{5,10},{6,9},{7,8},{8,7},{9,6},... | collective-permute-start | bytes 221192 | tf_op jit(solution)/shard_map/ppermute | solution.py:18
Sparse Core Ops, SparseCore 0:
  78.0 71.2 reduce-scatter.3
